TPU v7x, 32 devices: a whole 2x2x4 slice. The times are simulated.
32 devices in a mesh: mode: 8 (over y, x, core), wave: 4 (over z).
Axes of the slice: x: 2, y: 2, z: 4, core: 2. Of those that a mesh axis runs over, the one named last changes fastest.
Arguments:
- field_in: bfloat16 [4, 8, 2, 512, 512], P('wave', 'mode'), may hold values from -6 to 6
- target: bfloat16 [4, 8, 2, 512, 512], P('wave', 'mode'), may hold values from -6 to 6
- mask_old: bfloat16 [2, 512, 512], replicated, may hold values from -1 to 1
- scales: float32 [4], P('wave'), may hold values from 0.5 to 2
Outputs:
- mask_one: bfloat16 [2, 512, 512], P(None, 'mode')
- mask_two: bfloat16 [2, 512, 512], P(None, 'mode')
All inputs are finite; a program needn't handle non-finite values.
Results may differ from a plain program's by a relative error of at most 0.013.
Values may be sent and summed in bfloat16 or wider, within the bound.
A program may use at most 64 MiB of HBM per device.

v0:
```python
import jax
import jax.numpy as jnp
from jax import lax
from jax.sharding import PartitionSpec as P


def chirp(scale, count):
    pos = jnp.arange(count, dtype=jnp.float32)
    diff = pos[:, None] - pos[None, :]
    angle = jnp.pi * scale * diff * diff / count
    factor = jnp.float32(count) ** (-0.5)
    return (
        (jnp.cos(angle) * factor).astype(jnp.bfloat16),
        (jnp.sin(angle) * factor).astype(jnp.bfloat16),
    )


def right_matrix(real_part, imag_part, sign):
    upper = jnp.concatenate([real_part, sign * imag_part], 1)
    lower = jnp.concatenate([-sign * imag_part, real_part], 1)
    return jnp.concatenate([upper, lower], 0)


def left_matrix(real_part, imag_part, sign):
    first = jnp.concatenate([real_part, sign * imag_part], 0)
    second = jnp.concatenate([-sign * imag_part, real_part], 0)
    return jnp.stack([first, second], 0)


def right_product(field_re, field_im, right):
    joined = jnp.concatenate([field_re, field_im], -1)
    return jnp.einsum("brk,kc->brc", joined, right, preferred_element_type=jnp.float32).astype(
        jnp.bfloat16
    )


def left_product(middle, left):
    batch = middle.shape[0]
    count = middle.shape[1]
    shaped = middle.reshape(batch, count, 2, count)
    result = jnp.einsum("pqk,bkpc->bqc", left, shaped, preferred_element_type=jnp.float32)
    return (result[:, :count], result[:, count:])


def phasor_rows(total, power_sum, count):
    power = power_sum / (count * count)
    real_part = total[:, :count]
    imag_part = total[:, count:]
    factor = lax.rsqrt(real_part * real_part + imag_part * imag_part + power + 1e-06)
    return jnp.concatenate([real_part * factor, imag_part * factor], -1).astype(jnp.bfloat16)


def as_output(mask_part, count):
    return jnp.stack([mask_part[:, :count], mask_part[:, count:]], 0)


def whole_mask(term):
    total = lax.psum(term, ("mode", "wave"))
    return phasor_rows(total, jnp.sum(total * total), term.shape[1] // 2)


def local(field_in, target, mask_old, scales):
    count = field_in.shape[-1]
    row_count = count // lax.axis_size("mode")
    kernel_re, kernel_im = chirp(scales[0], count)
    f_re = field_in[0, :, 0]
    f_im = field_in[0, :, 1]
    b_re = target[0, :, 0].astype(jnp.float32)
    b_im = target[0, :, 1].astype(jnp.float32)
    old_re = mask_old[0].astype(jnp.float32)
    old_im = mask_old[1].astype(jnp.float32)
    c_re = (b_re * old_re + b_im * old_im).astype(jnp.bfloat16)
    c_im = (b_im * old_re - b_re * old_im).astype(jnp.bfloat16)
    middle = right_product(c_re, c_im, right_matrix(kernel_re, kernel_im, -1.0))
    back_re, back_im = left_product(middle, left_matrix(kernel_re, kernel_im, -1.0))
    fr32 = f_re.astype(jnp.float32)
    fi32 = f_im.astype(jnp.float32)
    term_one = jnp.concatenate(
        [jnp.sum(back_re * fr32 + back_im * fi32, 0), jnp.sum(back_im * fr32 - back_re * fi32, 0)],
        -1,
    )
    forward_right = right_matrix(kernel_re, kernel_im, 1.0)
    mask_full = whole_mask(term_one)
    new_re = mask_full[:, :count].astype(jnp.float32)
    new_im = mask_full[:, count:].astype(jnp.float32)
    g_re = (fr32 * new_re - fi32 * new_im).astype(jnp.bfloat16)
    g_im = (fr32 * new_im + fi32 * new_re).astype(jnp.bfloat16)
    ahead_mid = right_product(g_re, g_im, forward_right)
    first_rows = lax.dynamic_slice_in_dim(
        mask_full, lax.axis_index("mode") * row_count, row_count, 0
    )
    ahead_re, ahead_im = left_product(ahead_mid, left_matrix(kernel_re, kernel_im, 1.0))
    term_two = jnp.concatenate(
        [
            jnp.sum(b_re * ahead_re + b_im * ahead_im, 0),
            jnp.sum(b_im * ahead_re - b_re * ahead_im, 0),
        ],
        -1,
    )
    second_full = whole_mask(term_two)
    second_rows = lax.dynamic_slice_in_dim(
        second_full, lax.axis_index("mode") * row_count, row_count, 0
    )
    return (as_output(first_rows, count), as_output(second_rows, count))


def solution(mesh):
    in_specs = (
        P("wave", "mode", None, None, None),
        P("wave", "mode", None, None, None),
        P(),
        P("wave"),
    )
    out_specs = (P(None, "mode", None), P(None, "mode", None))
    return jax.shard_map(local, mesh=mesh, in_specs=in_specs, out_specs=out_specs, check_vma=False)
```

profile of v0, /device:TPU:0, one launch (start us, length us, event | category | flops | bytes accessed | tf_op | source)
XLA Modules:
  0.0 331.8 jit_solution(15147888423116012194)
XLA Ops:
  7.9 3.8 %broadcast_multiply_fusion = bf16[512,512]{1,0:T(8,128)(2,1)S(1)} fusion(f32[]{:T(128)} %bitcast.5), kind=kLoop, calls=%fused_computation.98 | loop fusion | flops 2621440 | bytes 524292 | tf_op jit(solution)/shard_map/mul | solution.py:19
  11.8 4.4 %multiply_convert_fusion.4 = bf16[512,512]{1,0:T(8,128)(2,1)} fusion(f32[]{:T(128)} %bitcast.5), kind=kLoop, calls=%fused_computation.90 | loop fusion | flops 1572864 | bytes 524292 | tf_op jit(solution)/shard_map/convert_element_type | solution.py:14
  16.2 4.4 %multiply_convert_fusion.5 = bf16[512,512]{1,0:T(8,128)(2,1)} fusion(f32[]{:T(128)} %bitcast.5), kind=kLoop, calls=%fused_computation.91 | loop fusion | flops 1572864 | bytes 524292 | tf_op jit(solution)/shard_map/convert_element_type | solution.py:13
  20.6 0.2 copy.18
  21.1 1.5 fusion.72
  23.0 3.7 %fusion.41 = (bf16[1,1024,512]{2,1,0:T(8,128)(2,1)}, bf16[1,1024,512]{2,1,0:T(8,128)(2,1)}, bf16[1,1024,512]{2,1,0:T(8,128)(2,1)}, bf16[1,1024,512]{2,1,0:T(8,128)(2,1)}) fusion(bf16[512,512]{1,0:T(8,128)(2,1)} %multiply_convert_fusion.5, bf16[512,512]{1,0:T(8,128)(2,1)} %multiply_convert_fusion.4, bf16[512,512]{1,0:T(8,128)(2,1)S(1)} %broadcast_multiply_fusion), kind=kLoop, calls=%fused_computation.56 | loop fusion | flops 7340032 | bytes 5767168 | tf_op jit(solution)/shard_map/stack | solution.py:27
  26.7 0.4 fusion.52
  27.1 0.6 copy-done.12
  27.9 1.3 fusion.27
  29.2 1.3 copy.16
  31.0 0.8 copy-done.18
  31.8 2.8 fusion.21
  34.6 0.4 fusion.47
  35.0 1.5 pad_maximum_fusion.6
  36.6 0.2 all-reduce.5.cloned.1.call-start
  36.8 136.4 %all-reduce.3.cloned.1.call-done = f32[512,1024]{0,1:T(8,128)} async-done(((f32[512,1024]{0,1:T(8,128)}), f32[512,1024]{0,1:T(8,128)}) %all-reduce.3.cloned.1.call-update) | async-done | bytes 2097168 | tf_op jit(solution)/shard_map/psum | solution.py:58
  173.2 2.9 multiply_reduce_fusion.1
  176.8 0.5 fusion.64
  177.4 0.3 fusion.63
  177.6 0.5 copy-done.2
  178.3 0.4 copy-done.11
  179.1 1.3 fusion.24
  180.4 0.5 copy.17
  180.9 0.7 copy-done.19
  181.6 2.6 fusion.18
  184.2 0.4 fusion.56
  184.6 1.5 pad_maximum_fusion.7
  186.1 132.8 %all-reduce.5.cloned.1.call-done = f32[512,1024]{0,1:T(8,128)} async-done(((f32[512,1024]{0,1:T(8,128)}), f32[512,1024]{0,1:T(8,128)}) %all-reduce.5.cloned.1.call-update) | async-done | bytes 2097168 | tf_op jit(solution)/shard_map/psum | solution.py:58
  318.9 2.9 multiply_reduce_fusion
  322.5 0.3 multiply_convert_fusion
  323.3 0.8 copy.15
  324.2 0.8 copy.14
  (50 shorter events, 2.5 us)
Async XLA Ops:
  7.2 13.4 %copy-start.16 = (bf16[1,1,2,512,512]{4,3,2,1,0:T(8,128)(2,1)S(1)}, bf16[1,1,2,512,512]{4,3,2,1,0:T(8,128)(2,1)}, u32[]{:S(2)}) copy-start(bf16[1,1,2,512,512]{4,3,2,1,0:T(8,128)(2,1)} %param.5) | copy-start | bytes 3145732
  7.2 166.1 %all-reduce.3.cloned.1.call-start = ((), (), s32[]{:S(2)}) async-start(), calls=%async_computation | async-start | bytes 4194304 | tf_op jit(solution)/shard_map/psum | solution.py:58
  11.7 15.4 %copy-start.10 = (bf16[512,512]{1,0:T(8,128)(2,1)}, bf16[512,512]{1,0:T(8,128)(2,1)S(1)}, u32[]{:S(2)}) copy-start(bf16[512,512]{1,0:T(8,128)(2,1)S(1)} %broadcast_multiply_fusion) | copy-start | bytes 1572868
  20.8 5.9 %copy-start.6 = (bf16[1,1,1,512,512]{3,4,2,1,0:T(8,128)(2,1)}, bf16[1,1,1,512,512]{3,4,2,1,0:T(8,128)(2,1)S(1)}, u32[]{:S(2)}) copy-start(bf16[1,1,1,512,512]{3,4,2,1,0:T(8,128)(2,1)S(1)} %copy.18) | copy-start | bytes 1572868
  21.0 5.6 %copy-start.8 = (bf16[1,1,1,512,512]{3,4,2,1,0:T(8,128)(2,1)}, bf16[1,1,1,512,512]{3,4,2,1,0:T(8,128)(2,1)S(1)}, u32[]{:S(2)}) copy-start(bf16[1,1,1,512,512]{3,4,2,1,0:T(8,128)(2,1)S(1)} %copy.20) | copy-start | bytes 1572868
  26.7 1.0 copy-start.12
  26.7 1.2 copy-start.14
  29.2 1.3 copy-start.17
  30.6 1.2 copy-start.18
  36.6 282.3 %all-reduce.5.cloned.1.call-start = ((), (), s32[]{:S(2)}) async-start(), calls=%async_computation.1 | async-start | bytes 4194304 | tf_op jit(solution)/shard_map/psum | solution.py:58
  173.2 3.5 %copy-start = (f32[512,1024]{0,1:T(8,128)S(1)}, f32[512,1024]{0,1:T(8,128)}, u32[]{:S(2)}) copy-start(f32[512,1024]{0,1:T(8,128)} %all-reduce.3.cloned.1.call-done) | copy-start | bytes 6291460
  177.3 0.8 copy-start.2
  177.3 1.0 copy-start.4
  177.3 1.4 copy-start.11
  177.3 1.6 copy-start.13
  177.4 1.7 copy-start.15
  180.3 1.2 copy-start.19
  181.6 2.6 copy-start.7
  181.6 2.6 copy-start.9
  318.9 3.6 %copy-start.1 = (f32[512,1024]{0,1:T(8,128)S(1)}, f32[512,1024]{0,1:T(8,128)}, u32[]{:S(2)}) copy-start(f32[512,1024]{0,1:T(8,128)} %all-reduce.5.cloned.1.call-done) | copy-start | bytes 6291460
  321.8 1.1 copy-start.3
  321.8 1.2 copy-start.5
Sparse Core Ops, SparseCore 0:
  36.7 136.4 all-reduce.2
  186.2 132.6 all-reduce.4
where the time goes:
time: 332 us
  waiting for transfers between devices  269 us (81%)
  other arithmetic  27.7 us (8%)
  between operations  16.5 us (5%)
  local copies, waits for them, and re-layouts  10.2 us (3%)
  matrix products  7.94 us (2%)
    psum x2, waiting for transfers between devices, whole_mask(): total = lax.psum(term, ('mode', 'wave'))  269 us
    unnamed x48, local copies, waits for them, and re-layouts  6.69 us
  transfers between devices with their start and end apart: 2, of which 2 were waited for; matrix products, arithmetic and copies ran while one was open for 0% of the time, Pallas kernels for 0%

commit v1 on v0

--- a/solution.py
+++ b/solution.py
@@ -1,7 +1,361 @@
+import functools
+
 import jax
 import jax.numpy as jnp
 from jax import lax
+from jax.experimental import pallas as pl
+from jax.experimental.pallas import tpu as pltpu
 from jax.sharding import PartitionSpec as P
+
+MESH = pl.DeviceIdType.MESH
+F32 = jnp.float32
+BF16 = jnp.bfloat16
+SUB = 16
+LANES = 128
+
+
+def build_right(scale, right, count):
+    wide = 2 * count
+    row = lax.broadcasted_iota(jnp.int32, (SUB, wide), 0)
+    col = lax.broadcasted_iota(jnp.int32, (SUB, wide), 1)
+    diff = (row - col + count).astype(F32)
+    angle = (jnp.pi * scale) * diff * diff / count
+    factor = float(count) ** (-0.5)
+    base_re = jnp.cos(angle) * factor
+    base_im = jnp.sin(angle) * factor
+    for shift in range(0, LANES, SUB):
+        re = (pltpu.roll(base_re, shift, 1) if shift else base_re).astype(BF16)
+        im = (pltpu.roll(base_im, shift, 1) if shift else base_im).astype(BF16)
+        for hop in range(count // LANES):
+            top = hop * LANES + shift
+            begin = count - hop * LANES
+            k_re = re[:, begin : begin + count]
+            k_im = im[:, begin : begin + count]
+            right[pl.ds(top, SUB), pl.ds(0, count)] = k_re
+            right[pl.ds(top, SUB), pl.ds(count, count)] = k_im
+            right[pl.ds(count + top, SUB), pl.ds(0, count)] = -k_im
+            right[pl.ds(count + top, SUB), pl.ds(count, count)] = k_re
+
+
+def kernel(
+    modes,
+    waves,
+    scale_ref,
+    field,
+    target,
+    old,
+    out_one,
+    out_two,
+    right,
+    joined,
+    middle,
+    part,
+    core_in,
+    chip_out,
+    chip_in,
+    wave_out,
+    wave_in,
+    whole,
+    last,
+    power_out,
+    power_in,
+    power_out2,
+    power_in2,
+    core_s,
+    core_r,
+    chip_s,
+    chip_r,
+    wave_s,
+    wave_r,
+    gw_s,
+    gw_r,
+    gx_s,
+    gx_r,
+    gc_s,
+    gc_r,
+    pm_s,
+    pm_r,
+    pw_s,
+    pw_r,
+):
+    count = field.shape[-1]
+    chips = modes // 2
+    rows = count // modes
+    piece = rows // waves
+    mode = lax.axis_index("mode")
+    wave = lax.axis_index("wave")
+    core = lax.rem(mode, 2)
+    chip = lax.div(mode, 2)
+    other = 1 - core
+
+    barrier = pltpu.get_barrier_semaphore()
+    for step in range(1, modes):
+        pl.semaphore_signal(
+            barrier, inc=1, device_id={"mode": lax.rem(mode + step, modes)}, device_id_type=MESH
+        )
+    for step in range(1, waves):
+        pl.semaphore_signal(
+            barrier, inc=1, device_id={"wave": lax.rem(wave + step, waves)}, device_id_type=MESH
+        )
+
+    def send(src, dst, s_sem, r_sem, to):
+        copy = pltpu.make_async_remote_copy(
+            src_ref=src, dst_ref=dst, send_sem=s_sem, recv_sem=r_sem, device_id=to, device_id_type=MESH
+        )
+        copy.start()
+        return copy
+
+    pending = []
+
+    def right_product():
+        for half, low in ((0, count), (1, 0)):
+            middle[pl.ds(low, count), :] = jnp.dot(
+                joined[...], right[:, pl.ds(half * count, count)], preferred_element_type=F32
+            ).astype(BF16)
+
+    def left_half(which, term):
+        starts = [pl.multiple_of((2 * q + which) * rows, rows) for q in range(chips)]
+        lhs = jnp.concatenate(
+            [right[pl.ds(s, rows), :] for s in starts]
+            + [right[pl.ds(pl.multiple_of(count + s, rows), rows), :] for s in starts],
+            0,
+        )
+        result = jnp.dot(lhs, middle[...], preferred_element_type=F32)
+        for q in range(chips):
+            im = result[q * rows : (q + 1) * rows]
+            re = result[(chips + q) * rows : (chips + q + 1) * rows]
+            at = pl.ds(starts[q], rows)
+            term_re, term_im = term(re, im, at)
+            part[which, q, :, pl.ds(0, count)] = term_re.astype(BF16)
+            part[which, q, :, pl.ds(count, count)] = term_im.astype(BF16)
+
+    def reduce_scatter(trip, term, ready):
+        left_half(other, term)
+        ready()
+        crossing = send(
+            part.at[other], core_in.at[trip], core_s.at[trip], core_r.at[trip], {"mode": 2 * chip + other}
+        )
+        left_half(core, term)
+        crossing.wait_recv()
+        copies = []
+        for step in range(1, chips):
+            to = lax.rem(chip + step, chips)
+            chip_out[trip, step] = (
+                part[core, to].astype(F32) + core_in[trip, to].astype(F32)
+            ).astype(BF16)
+            copies.append(
+                send(
+                    chip_out.at[trip, step],
+                    chip_in.at[trip, step],
+                    chip_s.at[trip, step],
+                    chip_r.at[trip, step],
+                    {"mode": 2 * to + core},
+                )
+            )
+        total = part[core, chip].astype(F32) + core_in[trip, chip].astype(F32)
+        for step, copy in enumerate(copies, 1):
+            copy.wait_recv()
+            total = total + chip_in[trip, step].astype(F32)
+        wave_out[trip] = total.astype(BF16).reshape(waves, piece, 2 * count)
+        hops = []
+        for step in range(1, waves):
+            to = lax.rem(wave + step, waves)
+            hops.append(
+                send(
+                    wave_out.at[trip, to],
+                    wave_in.at[trip, step],
+                    wave_s.at[trip, step],
+                    wave_r.at[trip, step],
+                    {"wave": to},
+                )
+            )
+        result = wave_out[trip, wave].astype(F32)
+        for step, copy in enumerate(hops, 1):
+            copy.wait_recv()
+            result = result + wave_in[trip, step].astype(F32)
+        pending.extend([crossing] + copies + hops)
+        return result
+
+    def phasor(block, power):
+        re = block[:, :count]
+        im = block[:, count:]
+        factor = lax.rsqrt(re * re + im * im + power + 1e-06)
+        return (re * factor).astype(BF16), (im * factor).astype(BF16)
+
+    build_right(scale_ref[0], right, count)
+
+    t_re = target[0].astype(F32)
+    t_im = target[1].astype(F32)
+    o_re = old[0].astype(F32)
+    o_im = old[1].astype(F32)
+    joined[:, pl.ds(0, count)] = (t_re * o_re + t_im * o_im).astype(BF16)
+    joined[:, pl.ds(count, count)] = (t_re * o_im - t_im * o_re).astype(BF16)
+    right_product()
+
+    def term_one(re, im, at):
+        f_re = field[0, at, :].astype(F32)
+        f_im = field[1, at, :].astype(F32)
+        return re * f_re - im * f_im, -(re * f_im + im * f_re)
+
+    def entered():
+        pl.semaphore_wait(barrier, modes - 1 + waves - 1)
+
+    margin = reduce_scatter(0, term_one, entered)
+
+    at = pl.ds(pl.multiple_of(wave * piece, piece), piece)
+    whole[core, chip, at, :] = margin.astype(BF16)
+    own = whole.at[core, chip, at]
+    hops = [
+        send(own, own, gw_s.at[step], gw_r.at[step], {"wave": lax.rem(wave + step, waves)})
+        for step in range(1, waves)
+    ]
+    for copy in hops:
+        copy.wait_recv()
+    block = whole.at[core, chip]
+    fans = [
+        send(block, block, gx_s.at[step], gx_r.at[step], {"mode": 2 * lax.rem(chip + step, chips) + core})
+        for step in range(1, chips)
+    ]
+    across = [send(block, block, gc_s.at[0], gc_r.at[0], {"mode": 2 * chip + other})]
+    for step, copy in enumerate(fans, 1):
+        copy.wait_recv()
+        came = whole.at[core, lax.rem(chip - step + chips, chips)]
+        across.append(send(came, came, gc_s.at[step], gc_r.at[step], {"mode": 2 * chip + other}))
+    for copy in across:
+        copy.wait_recv()
+    pending.extend(hops + fans + across)
+
+    squares = jnp.zeros((8, 2 * count), F32)
+    for c in range(2):
+        for q in range(chips):
+            block_f = whole[c, q].astype(F32)
+            squares = squares + jnp.sum((block_f * block_f).reshape(rows // 8, 8, 2 * count), 0)
+    power = jnp.sum(squares, keepdims=True) / (count * count)
+    for c in range(2):
+        for q in range(chips):
+            low = (2 * q + c) * rows
+            m_re, m_im = phasor(whole[c, q].astype(F32), power)
+            n_re = m_re.astype(F32)
+            n_im = m_im.astype(F32)
+            f_re = field[0, pl.ds(low, rows), :].astype(F32)
+            f_im = field[1, pl.ds(low, rows), :].astype(F32)
+            joined[pl.ds(low, rows), pl.ds(0, count)] = (f_re * n_re - f_im * n_im).astype(BF16)
+            joined[pl.ds(low, rows), pl.ds(count, count)] = (f_re * n_im + f_im * n_re).astype(BF16)
+    right_product()
+    m_re, m_im = phasor(whole[core, chip].astype(F32), power)
+    out_one[0] = m_re
+    out_one[1] = m_im
+
+    def term_two(re, im, at):
+        b_re = target[0, at, :].astype(F32)
+        b_im = target[1, at, :].astype(F32)
+        return b_re * re + b_im * im, b_im * re - b_re * im
+
+    for copy in pending:
+        copy.wait_send()
+    pending.clear()
+    margin = reduce_scatter(1, term_two, lambda: None)
+    squares = jnp.sum((margin * margin).reshape(piece // 8, 8, 2 * count), 0)
+    tile = squares[:, :LANES]
+    for low in range(LANES, 2 * count, LANES):
+        tile = tile + squares[:, low : low + LANES]
+    power_out[...] = tile
+    tiles = [
+        send(
+            power_out,
+            power_in.at[step],
+            pm_s.at[step],
+            pm_r.at[step],
+            {"mode": lax.rem(mode + step, modes)},
+        )
+        for step in range(1, modes)
+    ]
+    last[at, :] = margin.astype(BF16)
+    own = last.at[at]
+    hops = [
+        send(own, own, gw_s.at[waves + step], gw_r.at[waves + step], {"wave": lax.rem(wave + step, waves)})
+        for step in range(1, waves)
+    ]
+    for step, copy in enumerate(tiles, 1):
+        copy.wait_recv()
+        tile = tile + power_in[step]
+    power_out2[...] = tile
+    tiles2 = [
+        send(
+            power_out2,
+            power_in2.at[step],
+            pw_s.at[step],
+            pw_r.at[step],
+            {"wave": lax.rem(wave + step, waves)},
+        )
+        for step in range(1, waves)
+    ]
+    for step, copy in enumerate(tiles2, 1):
+        copy.wait_recv()
+        tile = tile + power_in2[step]
+    power = jnp.sum(tile, keepdims=True) / (count * count)
+    for copy in hops:
+        copy.wait_recv()
+    m_re, m_im = phasor(last[...].astype(F32), power)
+    out_two[0] = m_re
+    out_two[1] = m_im
+    for copy in pending + tiles + hops + tiles2:
+        copy.wait_send()
+
+
+def fused(field_in, target, mask_old, scales):
+    modes = lax.axis_size("mode")
+    waves = lax.axis_size("wave")
+    count = field_in.shape[-1]
+    chips = modes // 2
+    rows = count // modes
+    piece = rows // waves
+    dma = pltpu.SemaphoreType.DMA
+    out = jax.ShapeDtypeStruct((2, rows, count), BF16)
+    vmem = pl.BlockSpec(memory_space=pltpu.VMEM)
+    return pl.pallas_call(
+        functools.partial(kernel, modes, waves),
+        out_shape=(out, out),
+        in_specs=[pl.BlockSpec(memory_space=pltpu.SMEM), vmem, vmem, vmem],
+        out_specs=(vmem, vmem),
+        scratch_shapes=[
+            pltpu.VMEM((2 * count, 2 * count), BF16),
+            pltpu.VMEM((count, 2 * count), BF16),
+            pltpu.VMEM((2 * count, count), BF16),
+            pltpu.VMEM((2, chips, rows, 2 * count), BF16),
+            pltpu.VMEM((2, chips, rows, 2 * count), BF16),
+            pltpu.VMEM((2, chips, rows, 2 * count), BF16),
+            pltpu.VMEM((2, chips, rows, 2 * count), BF16),
+            pltpu.VMEM((2, waves, piece, 2 * count), BF16),
+            pltpu.VMEM((2, waves, piece, 2 * count), BF16),
+            pltpu.VMEM((2, chips, rows, 2 * count), BF16),
+            pltpu.VMEM((rows, 2 * count), BF16),
+            pltpu.VMEM((8, LANES), F32),
+            pltpu.VMEM((modes, 8, LANES), F32),
+            pltpu.VMEM((8, LANES), F32),
+            pltpu.VMEM((waves, 8, LANES), F32),
+            dma((2,)),
+            dma((2,)),
+            dma((2, chips)),
+            dma((2, chips)),
+            dma((2, waves)),
+            dma((2, waves)),
+            dma((2 * waves,)),
+            dma((2 * waves,)),
+            dma((chips,)),
+            dma((chips,)),
+            dma((chips,)),
+            dma((chips,)),
+            dma((modes,)),
+            dma((modes,)),
+            dma((waves,)),
+            dma((waves,)),
+        ],
+        compiler_params=pltpu.CompilerParams(
+            collective_id=0, has_side_effects=True, vmem_limit_bytes=48 * 1024 * 1024
+        ),
+        cost_estimate=pl.CostEstimate(flops=16 * count**3 * 2, bytes_accessed=12 * count**2, transcendentals=0),
+    )(scales, field_in[0, 0], target[0, 0], mask_old)
 
 
 def chirp(scale, count):
@@ -112,4 +466,15 @@
         P("wave"),
     )
     out_specs = (P(None, "mode", None), P(None, "mode", None))
-    return jax.shard_map(local, mesh=mesh, in_specs=in_specs, out_specs=out_specs, check_vma=False)
+    modes, waves = mesh.shape["mode"], mesh.shape["wave"]
+
+    def step(field_in, target, mask_old, scales):
+        count = field_in.shape[-1]
+        single = field_in.shape[0] == waves and field_in.shape[1] == modes
+        fits = modes % 2 == 0 and count % (modes * waves * SUB) == 0 and count % LANES == 0
+        body = fused if single and fits else local
+        return jax.shard_map(body, mesh=mesh, in_specs=in_specs, out_specs=out_specs, check_vma=False)(
+            field_in, target, mask_old, scales
+        )
+
+    return step

time: 332 us -> 61.5 us (0.19)
  waiting for transfers between devices: 269 us -> 0 us
  Pallas kernels: 0 us -> 55 us
  other arithmetic: 27.7 us -> 0 us
  between operations: 16.5 us -> 1.3 us
  matrix products: 7.94 us -> 0 us
  local copies, waits for them, and re-layouts: 10.2 us -> 4.98 us
    psum x2 -> x0, waiting for transfers between devices: 269 us -> none  [whole_mask(): total = lax.psum(term, ('mode', 'wave'))]
    pallas_call x0 -> x1, Pallas kernels: none -> 55 us  [fused(): pl.pallas_call(functools.partial(kernel, modes, waves), out_shape=(out, o...]
    convert_element_type x5 -> x0, other arithmetic: 9.96 us -> none  [the longest x1 4.41 us: chirp(): (jnp.sin(angle) * factor).astype(jnp.bfloat16)]
    dot_general x4 -> x0, matrix products: 7.94 us -> none  [the longest x2 5.41 us: left_product(): jnp.einsum('pqk,bkpc->bqc', left, shaped, preferred_element_type=jnp.floa...]
    reduce_sum x4 -> x0, other arithmetic: 6.52 us -> none  [the longest x2 5.77 us: whole_mask(): return phasor_rows(total, jnp.sum(total * total), term.shape[1] // 2)]
    another operation x4 -> x0, other arithmetic: 4.16 us -> none  [the longest x1 3.73 us: left_matrix(): return jnp.stack([first, second], 0)]
    mul x1 -> x0, other arithmetic: 3.79 us -> none  [right_matrix(): upper = jnp.concatenate([real_part, sign * imag_part], 1)]
    unnamed x48 -> x8, local copies, waits for them, and re-layouts: 6.69 us -> 4.98 us
  transfers between devices with their start and end apart: 2 -> 0, of which waited for: 2 -> 0; matrix products, arithmetic and copies ran while one was open for 0% -> 0% of each run, Pallas kernels for 0% -> 0%
where the time goes in v1:
time: 61.5 us; the launch traced here: 61.2 us
  Pallas kernels  55 us (89%)
  local copies, waits for them, and re-layouts  4.98 us (8%)
  between operations  1.3 us (2%)
    pallas_call x1, Pallas kernels, fused(): pl.pallas_call(functools.partial(kernel, modes, waves), out_shape=(out, o...  55 us
    unnamed x8, local copies, waits for them, and re-layouts  4.98 us

profile of v1, /device:TPU:0, one launch (start us, length us, event | category | flops | bytes accessed | tf_op | source)
XLA Modules:
  0.0 61.2 jit_solution(4597410995416626364)
XLA Ops:
  1.3 0.0 copy-start
  1.3 1.2 %copy-done = bf16[1,1,2,512,512]{4,3,2,1,0:T(8,128)(2,1)S(1)} copy-done((bf16[1,1,2,512,512]{4,3,2,1,0:T(8,128)(2,1)S(1)}, bf16[1,1,2,512,512]{4,3,2,1,0:T(8,128)(2,1)}, u32[]{:S(2)}) %copy-start) | copy-done | bytes 1048600
  2.5 0.0 copy-start.1
  2.5 1.2 %copy-done.1 = bf16[1,1,2,512,512]{4,3,2,1,0:T(8,128)(2,1)S(1)} copy-done((bf16[1,1,2,512,512]{4,3,2,1,0:T(8,128)(2,1)S(1)}, bf16[1,1,2,512,512]{4,3,2,1,0:T(8,128)(2,1)}, u32[]{:S(2)}) %copy-start.1) | copy-done | bytes 1048600
  3.7 0.0 copy-start.2
  3.7 1.2 %copy-done.2 = bf16[2,512,512]{2,1,0:T(8,128)(2,1)S(1)} copy-done((bf16[2,512,512]{2,1,0:T(8,128)(2,1)S(1)}, bf16[2,512,512]{2,1,0:T(8,128)(2,1)}, u32[]{:S(2)}) %copy-start.2) | copy-done | bytes 1048600
  5.0 55.0 %shard_map.59 = (bf16[2,64,512]{2,1,0:T(8,128)(2,1)S(1)}, bf16[2,64,512]{2,1,0:T(8,128)(2,1)S(1)}) custom-call(f32[1]{0:T(128)S(6)} %copy.8.scale_ref, bf16[2,512,512]{2,1,0:T(8,128)(2,1)S(1)} %bitcast.2, bf16[2,512,512]{2,1,0:T(8,128)(2,1)S(1)} %bitcast.3, bf16[2,512,512]{2,1,0:T(8,128)(2,1)S(1)} %copy-done.2), custom_call_target="tpu_custom_call" | custom-call | flops 4294967296 | bytes 3145728 | tf_op jit(solution)/shard_map/pallas_call | solution.py:316
  59.9 0.7 %copy.9 = bf16[2,64,512]{2,1,0:T(8,128)(2,1)} copy(bf16[2,64,512]{2,1,0:T(8,128)(2,1)S(1)} %get-tuple-element.4) | data formatting | bytes 262144
  60.6 0.7 %copy.10 = bf16[2,64,512]{2,1,0:T(8,128)(2,1)} copy(bf16[2,64,512]{2,1,0:T(8,128)(2,1)S(1)} %get-tuple-element.5) | data formatting | bytes 262144
Async XLA Ops:
  1.3 1.2 %copy-start = (bf16[1,1,2,512,512]{4,3,2,1,0:T(8,128)(2,1)S(1)}, bf16[1,1,2,512,512]{4,3,2,1,0:T(8,128)(2,1)}, u32[]{:S(2)}) copy-start(bf16[1,1,2,512,512]{4,3,2,1,0:T(8,128)(2,1)} %param.4) | copy-start | bytes 3145732
  2.5 1.2 %copy-start.1 = (bf16[1,1,2,512,512]{4,3,2,1,0:T(8,128)(2,1)S(1)}, bf16[1,1,2,512,512]{4,3,2,1,0:T(8,128)(2,1)}, u32[]{:S(2)}) copy-start(bf16[1,1,2,512,512]{4,3,2,1,0:T(8,128)(2,1)} %param.5) | copy-start | bytes 3145732
  3.7 1.2 %copy-start.2 = (bf16[2,512,512]{2,1,0:T(8,128)(2,1)S(1)}, bf16[2,512,512]{2,1,0:T(8,128)(2,1)}, u32[]{:S(2)}) copy-start(bf16[2,512,512]{2,1,0:T(8,128)(2,1)} %old.1) | copy-start | bytes 3145732

commit v2 on v0

--- a/solution.py
+++ b/solution.py
@@ -1,7 +1,443 @@
+import functools
+
 import jax
 import jax.numpy as jnp
 from jax import lax
+from jax.experimental import pallas as pl
+from jax.experimental.pallas import tpu as pltpu
 from jax.sharding import PartitionSpec as P
+
+MESH = pl.DeviceIdType.MESH
+F32 = jnp.float32
+BF16 = jnp.bfloat16
+SUB = 16
+LANES = 128
+CUTS = 2
+
+
+def build_right(scale, right, count):
+    wide = 2 * count
+    row = lax.broadcasted_iota(jnp.int32, (SUB, wide), 0)
+    col = lax.broadcasted_iota(jnp.int32, (SUB, wide), 1)
+    diff = (row - col + count).astype(F32)
+    angle = (jnp.pi * scale) * diff * diff / count
+    factor = float(count) ** (-0.5)
+    base_re = jnp.cos(angle) * factor
+    base_im = jnp.sin(angle) * factor
+    for shift in range(0, LANES, SUB):
+        re = (pltpu.roll(base_re, shift, 1) if shift else base_re).astype(BF16)
+        im = (pltpu.roll(base_im, shift, 1) if shift else base_im).astype(BF16)
+        for hop in range(count // LANES):
+            top = hop * LANES + shift
+            begin = count - hop * LANES
+            k_re = re[:, begin : begin + count]
+            k_im = im[:, begin : begin + count]
+            right[pl.ds(top, SUB), pl.ds(0, count)] = k_re
+            right[pl.ds(top, SUB), pl.ds(count, count)] = k_im
+            right[pl.ds(count + top, SUB), pl.ds(0, count)] = -k_im
+            right[pl.ds(count + top, SUB), pl.ds(count, count)] = k_re
+
+
+def kernel(
+    modes,
+    waves,
+    scale_ref,
+    field_hbm,
+    target_hbm,
+    old_hbm,
+    out_one,
+    out_two,
+    field,
+    target,
+    old,
+    right,
+    joined,
+    middle,
+    part,
+    core_in,
+    chip_out,
+    chip_in,
+    wave_out,
+    wave_in,
+    whole,
+    last,
+    power_out,
+    power_in,
+    power_out2,
+    power_in2,
+    load_s,
+    core_s,
+    core_r,
+    chip_s,
+    chip_r,
+    wave_s,
+    wave_r,
+    gw_s,
+    gw_r,
+    gx_s,
+    gx_r,
+    gc_s,
+    gc_r,
+    pm_s,
+    pm_r,
+    pw_s,
+    pw_r,
+):
+    count = field.shape[-1]
+    chips = modes // 2
+    rows = count // modes
+    piece = rows // waves
+    width = count // CUTS
+    mode = lax.axis_index("mode")
+    wave = lax.axis_index("wave")
+    core = lax.rem(mode, 2)
+    chip = lax.div(mode, 2)
+    other = 1 - core
+
+    loads = [
+        pltpu.make_async_copy(src, dst, load_s.at[i])
+        for i, (src, dst) in enumerate(((target_hbm, target), (old_hbm, old), (field_hbm, field)))
+    ]
+    for copy in loads:
+        copy.start()
+
+    barrier = pltpu.get_barrier_semaphore()
+    for step in range(1, modes):
+        pl.semaphore_signal(
+            barrier, inc=1, device_id={"mode": lax.rem(mode + step, modes)}, device_id_type=MESH
+        )
+    for step in range(1, waves):
+        pl.semaphore_signal(
+            barrier, inc=1, device_id={"wave": lax.rem(wave + step, waves)}, device_id_type=MESH
+        )
+
+    pending = []
+
+    def send(src, dst, s_sem, r_sem, to):
+        copy = pltpu.make_async_remote_copy(
+            src_ref=src, dst_ref=dst, send_sem=s_sem, recv_sem=r_sem, device_id=to, device_id_type=MESH
+        )
+        copy.start()
+        pending.append(copy)
+        return copy
+
+    def starts_of(which):
+        return [pl.multiple_of((2 * q + which) * rows, rows) for q in range(chips)]
+
+    def right_rows(low, starts):
+        size = rows * len(starts)
+        for half, base in ((0, count), (1, 0)):
+            result = jnp.dot(
+                joined[pl.ds(low, size), :],
+                right[:, pl.ds(half * count, count)],
+                preferred_element_type=F32,
+            ).astype(BF16)
+            for q, start in enumerate(starts):
+                middle[pl.ds(pl.multiple_of(base + start, rows), rows), :] = result[q * rows : (q + 1) * rows]
+
+    def left_half(trip, cut, which, term):
+        starts = starts_of(which)
+        cols = pl.ds(cut * width, width)
+        lhs = jnp.concatenate(
+            [right[pl.ds(s, rows), :] for s in starts]
+            + [right[pl.ds(pl.multiple_of(count + s, rows), rows), :] for s in starts],
+            0,
+        )
+        result = jnp.dot(lhs, middle[:, cols], preferred_element_type=F32)
+        for q in range(chips):
+            im = result[q * rows : (q + 1) * rows]
+            re = result[(chips + q) * rows : (chips + q + 1) * rows]
+            term_re, term_im = term(re, im, pl.ds(starts[q], rows), cols)
+            part[trip, cut, which, q, :, pl.ds(0, width)] = term_re.astype(BF16)
+            part[trip, cut, which, q, :, pl.ds(width, width)] = term_im.astype(BF16)
+
+    def reduce_scatter(trip, term, ready, arrived):
+        fans = []
+        for cut in range(CUTS):
+            left_half(trip, cut, other, term)
+            if cut == 0:
+                ready()
+            crossing = send(
+                part.at[trip, cut, other],
+                core_in.at[trip, cut],
+                core_s.at[trip, cut],
+                core_r.at[trip, cut],
+                {"mode": 2 * chip + other},
+            )
+            left_half(trip, cut, core, term)
+            crossing.wait_recv()
+            fan = []
+            for step in range(1, chips):
+                to = lax.rem(chip + step, chips)
+                chip_out[trip, cut, step] = (
+                    part[trip, cut, core, to].astype(F32) + core_in[trip, cut, to].astype(F32)
+                ).astype(BF16)
+                fan.append(
+                    send(
+                        chip_out.at[trip, cut, step],
+                        chip_in.at[trip, cut, step],
+                        chip_s.at[trip, cut, step],
+                        chip_r.at[trip, cut, step],
+                        {"mode": 2 * to + core},
+                    )
+                )
+            fans.append(fan)
+        hops = []
+        for cut in range(CUTS):
+            total = part[trip, cut, core, chip].astype(F32) + core_in[trip, cut, chip].astype(F32)
+            for step, copy in enumerate(fans[cut], 1):
+                copy.wait_recv()
+                total = total + chip_in[trip, cut, step].astype(F32)
+            wave_out[trip, cut] = total.astype(BF16).reshape(waves, piece, 2 * width)
+            hop = []
+            for step in range(1, waves):
+                to = lax.rem(wave + step, waves)
+                hop.append(
+                    send(
+                        wave_out.at[trip, cut, to],
+                        wave_in.at[trip, cut, step],
+                        wave_s.at[trip, cut, step],
+                        wave_r.at[trip, cut, step],
+                        {"wave": to},
+                    )
+                )
+            hops.append(hop)
+        for cut in range(CUTS):
+            result = wave_out[trip, cut, wave].astype(F32)
+            for step, copy in enumerate(hops[cut], 1):
+                copy.wait_recv()
+                result = result + wave_in[trip, cut, step].astype(F32)
+            arrived(cut, result)
+
+    def folded(values):
+        squares = jnp.sum((values * values).reshape(piece // 8, 8, 2 * width), 0)
+        tile = squares[:, :LANES]
+        for low in range(LANES, 2 * width, LANES):
+            tile = tile + squares[:, low : low + LANES]
+        return tile
+
+    def power_over_modes(trip, tile):
+        power_out[trip] = tile
+        return [
+            send(
+                power_out.at[trip],
+                power_in.at[trip, step],
+                pm_s.at[trip, step],
+                pm_r.at[trip, step],
+                {"mode": lax.rem(mode + step, modes)},
+            )
+            for step in range(1, modes)
+        ]
+
+    def power_over_waves(trip, tile, copies):
+        for step, copy in enumerate(copies, 1):
+            copy.wait_recv()
+            tile = tile + power_in[trip, step]
+        power_out2[trip] = tile
+        return tile, [
+            send(
+                power_out2.at[trip],
+                power_in2.at[trip, step],
+                pw_s.at[trip, step],
+                pw_r.at[trip, step],
+                {"wave": lax.rem(wave + step, waves)},
+            )
+            for step in range(1, waves)
+        ]
+
+    def mean_power(trip, tile, copies):
+        for step, copy in enumerate(copies, 1):
+            copy.wait_recv()
+            tile = tile + power_in2[trip, step]
+        return jnp.sum(tile, keepdims=True) / (count * count)
+
+    def phasor(block, power):
+        re = block[:, :width].astype(F32)
+        im = block[:, width:].astype(F32)
+        factor = lax.rsqrt(re * re + im * im + power + 1e-06)
+        return (re * factor).astype(BF16), (im * factor).astype(BF16)
+
+    build_right(scale_ref[0], right, count)
+
+    loads[0].wait()
+    loads[1].wait()
+    t_re = target[0].astype(F32)
+    t_im = target[1].astype(F32)
+    o_re = old[0].astype(F32)
+    o_im = old[1].astype(F32)
+    joined[:, pl.ds(0, count)] = (t_re * o_re + t_im * o_im).astype(BF16)
+    joined[:, pl.ds(count, count)] = (t_re * o_im - t_im * o_re).astype(BF16)
+    right_rows(0, [q * rows for q in range(modes)])
+    loads[2].wait()
+
+    def term_one(re, im, at, cols):
+        f_re = field[0, at, cols].astype(F32)
+        f_im = field[1, at, cols].astype(F32)
+        return re * f_re - im * f_im, -(re * f_im + im * f_re)
+
+    def entered():
+        pl.semaphore_wait(barrier, modes - 1 + waves - 1)
+
+    mine = pl.ds(pl.multiple_of(wave * piece, piece), piece)
+    squares = []
+    hops = []
+
+    def spread(trip, cut, own, value):
+        own[...] = value.astype(BF16)
+        hops.append(
+            [
+                send(
+                    own,
+                    own,
+                    gw_s.at[trip, cut, step],
+                    gw_r.at[trip, cut, step],
+                    {"wave": lax.rem(wave + step, waves)},
+                )
+                for step in range(1, waves)
+            ]
+        )
+        squares.append(folded(value))
+
+    reduce_scatter(0, term_one, entered, lambda cut, v: spread(0, cut, whole.at[cut, core, chip, mine], v))
+    tile = sum(squares[1:], squares[0])
+    tiles = power_over_modes(0, tile)
+    fans = []
+    across = []
+    for cut in range(CUTS):
+        for copy in hops[cut]:
+            copy.wait_recv()
+        block = whole.at[cut, core, chip]
+        fans.append(
+            [
+                send(
+                    block,
+                    block,
+                    gx_s.at[cut, step],
+                    gx_r.at[cut, step],
+                    {"mode": 2 * lax.rem(chip + step, chips) + core},
+                )
+                for step in range(1, chips)
+            ]
+        )
+        across.append(send(block, block, gc_s.at[cut, 0], gc_r.at[cut, 0], {"mode": 2 * chip + other}))
+    tile, tiles2 = power_over_waves(0, tile, tiles)
+    for cut in range(CUTS):
+        for step, copy in enumerate(fans[cut], 1):
+            copy.wait_recv()
+            came = whole.at[cut, core, lax.rem(chip - step + chips, chips)]
+            across.append(
+                send(came, came, gc_s.at[cut, step], gc_r.at[cut, step], {"mode": 2 * chip + other})
+            )
+    power = mean_power(0, tile, tiles2)
+
+    def forward_half(which, low):
+        starts = starts_of(which)
+        for q, start in enumerate(starts):
+            at = pl.ds(low + q * rows, rows)
+            for cut in range(CUTS):
+                cols = pl.ds(cut * width, width)
+                m_re, m_im = phasor(whole[cut, which, q], power)
+                n_re = m_re.astype(F32)
+                n_im = m_im.astype(F32)
+                f_re = field[0, pl.ds(start, rows), cols].astype(F32)
+                f_im = field[1, pl.ds(start, rows), cols].astype(F32)
+                joined[at, cols] = (f_re * n_re - f_im * n_im).astype(BF16)
+                joined[at, pl.ds(count + cut * width, width)] = (f_re * n_im + f_im * n_re).astype(BF16)
+        right_rows(low, starts)
+
+    forward_half(core, 0)
+    for copy in across:
+        copy.wait_recv()
+    forward_half(other, count // 2)
+
+    def term_two(re, im, at, cols):
+        b_re = target[0, at, cols].astype(F32)
+        b_im = target[1, at, cols].astype(F32)
+        return b_re * re + b_im * im, b_im * re - b_re * im
+
+    squares.clear()
+    hops.clear()
+    reduce_scatter(1, term_two, lambda: None, lambda cut, v: spread(1, cut, last.at[cut, mine], v))
+    tile = sum(squares[1:], squares[0])
+    tiles = power_over_modes(1, tile)
+    for cut in range(CUTS):
+        cols = pl.ds(cut * width, width)
+        m_re, m_im = phasor(whole[cut, core, chip], power)
+        out_one[0, :, cols] = m_re
+        out_one[1, :, cols] = m_im
+    tile, tiles2 = power_over_waves(1, tile, tiles)
+    for hop in hops:
+        for copy in hop:
+            copy.wait_recv()
+    power = mean_power(1, tile, tiles2)
+    for cut in range(CUTS):
+        cols = pl.ds(cut * width, width)
+        m_re, m_im = phasor(last[cut], power)
+        out_two[0, :, cols] = m_re
+        out_two[1, :, cols] = m_im
+    for copy in pending:
+        copy.wait_send()
+
+
+def fused(field_in, target, mask_old, scales):
+    modes = lax.axis_size("mode")
+    waves = lax.axis_size("wave")
+    count = field_in.shape[-1]
+    chips = modes // 2
+    rows = count // modes
+    piece = rows // waves
+    wide = 2 * count // CUTS
+    dma = pltpu.SemaphoreType.DMA
+    out = jax.ShapeDtypeStruct((2, rows, count), BF16)
+    vmem = pl.BlockSpec(memory_space=pltpu.VMEM)
+    anywhere = pl.BlockSpec(memory_space=pl.ANY)
+    return pl.pallas_call(
+        functools.partial(kernel, modes, waves),
+        out_shape=(out, out),
+        in_specs=[pl.BlockSpec(memory_space=pltpu.SMEM), anywhere, anywhere, anywhere],
+        out_specs=(vmem, vmem),
+        scratch_shapes=[
+            pltpu.VMEM((2, count, count), BF16),
+            pltpu.VMEM((2, count, count), BF16),
+            pltpu.VMEM((2, count, count), BF16),
+            pltpu.VMEM((2 * count, 2 * count), BF16),
+            pltpu.VMEM((count, 2 * count), BF16),
+            pltpu.VMEM((2 * count, count), BF16),
+            pltpu.VMEM((2, CUTS, 2, chips, rows, wide), BF16),
+            pltpu.VMEM((2, CUTS, chips, rows, wide), BF16),
+            pltpu.VMEM((2, CUTS, chips, rows, wide), BF16),
+            pltpu.VMEM((2, CUTS, chips, rows, wide), BF16),
+            pltpu.VMEM((2, CUTS, waves, piece, wide), BF16),
+            pltpu.VMEM((2, CUTS, waves, piece, wide), BF16),
+            pltpu.VMEM((CUTS, 2, chips, rows, wide), BF16),
+            pltpu.VMEM((CUTS, rows, wide), BF16),
+            pltpu.VMEM((2, 8, LANES), F32),
+            pltpu.VMEM((2, modes, 8, LANES), F32),
+            pltpu.VMEM((2, 8, LANES), F32),
+            pltpu.VMEM((2, waves, 8, LANES), F32),
+            dma((3,)),
+            dma((2, CUTS)),
+            dma((2, CUTS)),
+            dma((2, CUTS, chips)),
+            dma((2, CUTS, chips)),
+            dma((2, CUTS, waves)),
+            dma((2, CUTS, waves)),
+            dma((2, CUTS, waves)),
+            dma((2, CUTS, waves)),
+            dma((CUTS, chips)),
+            dma((CUTS, chips)),
+            dma((CUTS, chips)),
+            dma((CUTS, chips)),
+            dma((2, modes)),
+            dma((2, modes)),
+            dma((2, waves)),
+            dma((2, waves)),
+        ],
+        compiler_params=pltpu.CompilerParams(
+            collective_id=0, has_side_effects=True, vmem_limit_bytes=56 * 1024 * 1024
+        ),
+        cost_estimate=pl.CostEstimate(flops=16 * count**3 * 2, bytes_accessed=12 * count**2, transcendentals=0),
+    )(scales, field_in[0, 0], target[0, 0], mask_old)
 
 
 def chirp(scale, count):
@@ -112,4 +548,15 @@
         P("wave"),
     )
     out_specs = (P(None, "mode", None), P(None, "mode", None))
-    return jax.shard_map(local, mesh=mesh, in_specs=in_specs, out_specs=out_specs, check_vma=False)
+    modes, waves = mesh.shape["mode"], mesh.shape["wave"]
+
+    def step(field_in, target, mask_old, scales):
+        count = field_in.shape[-1]
+        single = field_in.shape[0] == waves and field_in.shape[1] == modes
+        fits = modes % 2 == 0 and count % (modes * waves * SUB) == 0 and count % (CUTS * LANES) == 0
+        body = fused if single and fits else local
+        return jax.shard_map(body, mesh=mesh, in_specs=in_specs, out_specs=out_specs, check_vma=False)(
+            field_in, target, mask_old, scales
+        )
+
+    return step

time: 332 us -> 57.7 us (0.17)
  waiting for transfers between devices: 269 us -> 0 us
  Pallas kernels: 0 us -> 54 us
  other arithmetic: 27.7 us -> 0 us
  between operations: 16.5 us -> 1.29 us
  matrix products: 7.94 us -> 0 us
  local copies, waits for them, and re-layouts: 10.2 us -> 2.26 us
    psum x2 -> x0, waiting for transfers between devices: 269 us -> none  [whole_mask(): total = lax.psum(term, ('mode', 'wave'))]
    pallas_call x0 -> x1, Pallas kernels: none -> 54 us  [fused(): pl.pallas_call(functools.partial(kernel, modes, waves), out_shape=(out, o...]
    convert_element_type x5 -> x0, other arithmetic: 9.96 us -> none  [the longest x1 4.41 us: chirp(): (jnp.sin(angle) * factor).astype(jnp.bfloat16)]
    dot_general x4 -> x0, matrix products: 7.94 us -> none  [the longest x2 5.41 us: left_product(): jnp.einsum('pqk,bkpc->bqc', left, shaped, preferred_element_type=jnp.floa...]
    reduce_sum x4 -> x0, other arithmetic: 6.52 us -> none  [the longest x2 5.77 us: whole_mask(): return phasor_rows(total, jnp.sum(total * total), term.shape[1] // 2)]
    unnamed x48 -> x4, local copies, waits for them, and re-layouts: 6.69 us -> 2.26 us
    another operation x4 -> x0, other arithmetic: 4.16 us -> none  [the longest x1 3.73 us: left_matrix(): return jnp.stack([first, second], 0)]
    mul x1 -> x0, other arithmetic: 3.79 us -> none  [right_matrix(): upper = jnp.concatenate([real_part, sign * imag_part], 1)]
  transfers between devices with their start and end apart: 2 -> 0, of which waited for: 2 -> 0; matrix products, arithmetic and copies ran while one was open for 0% -> 0% of each run, Pallas kernels for 0% -> 0%
where the time goes in v2:
time: 57.7 us; the launch traced here: 57.6 us
  Pallas kernels  54 us (94%)
  local copies, waits for them, and re-layouts  2.26 us (4%)
  between operations  1.29 us (2%)
    pallas_call x1, Pallas kernels, fused(): pl.pallas_call(functools.partial(kernel, modes, waves), out_shape=(out, o...  54 us
    unnamed x4, local copies, waits for them, and re-layouts  2.26 us

profile of v2, /device:TPU:0, one launch (start us, length us, event | category | flops | bytes accessed | tf_op | source)
XLA Modules:
  0.0 57.6 jit_solution(2706764861586975561)
XLA Ops:
  1.3 54.0 %shard_map.59 = (bf16[2,64,512]{2,1,0:T(8,128)(2,1)}, bf16[2,64,512]{2,1,0:T(8,128)(2,1)}) custom-call(f32[1]{0:T(128)S(6)} %copy.8.scale_ref, bf16[2,512,512]{2,1,0:T(8,128)(2,1)} %bitcast.2, bf16[2,512,512]{2,1,0:T(8,128)(2,1)} %bitcast.3, bf16[2,512,512]{2,1,0:T(8,128)(2,1)} %old_hbm.1), custom_call_target="tpu_custom_call" | custom-call | flops 4294967296 | bytes 3145728 | tf_op jit(solution)/shard_map/pallas_call | solution.py:394
  55.3 0.0 copy-start
  55.3 1.6 %copy.9 = bf16[2,64,512]{2,1,0:T(8,128)(2,1)} copy(bf16[2,64,512]{2,1,0:T(8,128)(2,1)} %get-tuple-element.4) | data formatting | bytes 262144
  56.9 0.0 copy-done
  56.9 0.7 %copy.10 = bf16[2,64,512]{2,1,0:T(8,128)(2,1)} copy(bf16[2,64,512]{2,1,0:T(8,128)(2,1)S(1)} %copy-done) | data formatting | bytes 262144
Async XLA Ops:
  55.3 1.6 %copy-start = (bf16[2,64,512]{2,1,0:T(8,128)(2,1)S(1)}, bf16[2,64,512]{2,1,0:T(8,128)(2,1)}, u32[]{:S(2)}) copy-start(bf16[2,64,512]{2,1,0:T(8,128)(2,1)} %get-tuple-element.5) | copy-start | bytes 393220

commit v3 on v2

--- a/solution.py
+++ b/solution.py
@@ -12,18 +12,21 @@
 BF16 = jnp.bfloat16
 SUB = 16
 LANES = 128
-CUTS = 2
+CUTS = 1
 
 
 def build_right(scale, right, count):
     wide = 2 * count
-    row = lax.broadcasted_iota(jnp.int32, (SUB, wide), 0)
-    col = lax.broadcasted_iota(jnp.int32, (SUB, wide), 1)
+    half = SUB // 2
+    row = lax.broadcasted_iota(jnp.int32, (half, wide), 0)
+    col = lax.broadcasted_iota(jnp.int32, (half, wide), 1)
     diff = (row - col + count).astype(F32)
     angle = (jnp.pi * scale) * diff * diff / count
     factor = float(count) ** (-0.5)
-    base_re = jnp.cos(angle) * factor
-    base_im = jnp.sin(angle) * factor
+    top_re = jnp.cos(angle) * factor
+    top_im = jnp.sin(angle) * factor
+    base_re = jnp.concatenate([top_re, pltpu.roll(top_re, half, 1)], 0)
+    base_im = jnp.concatenate([top_im, pltpu.roll(top_im, half, 1)], 0)
     for shift in range(0, LANES, SUB):
         re = (pltpu.roll(base_re, shift, 1) if shift else base_re).astype(BF16)
         im = (pltpu.roll(base_im, shift, 1) if shift else base_im).astype(BF16)
@@ -95,8 +98,9 @@
     other = 1 - core
 
     loads = [
-        pltpu.make_async_copy(src, dst, load_s.at[i])
+        pltpu.make_async_copy(src.at[p], dst.at[p], load_s.at[2 * i + p])
         for i, (src, dst) in enumerate(((target_hbm, target), (old_hbm, old), (field_hbm, field)))
+        for p in range(2)
     ]
     for copy in loads:
         copy.start()
@@ -259,8 +263,8 @@
 
     build_right(scale_ref[0], right, count)
 
-    loads[0].wait()
-    loads[1].wait()
+    for copy in loads[:4]:
+        copy.wait()
     t_re = target[0].astype(F32)
     t_im = target[1].astype(F32)
     o_re = old[0].astype(F32)
@@ -268,7 +272,8 @@
     joined[:, pl.ds(0, count)] = (t_re * o_re + t_im * o_im).astype(BF16)
     joined[:, pl.ds(count, count)] = (t_re * o_im - t_im * o_re).astype(BF16)
     right_rows(0, [q * rows for q in range(modes)])
-    loads[2].wait()
+    for copy in loads[4:]:
+        copy.wait()
 
     def term_one(re, im, at, cols):
         f_re = field[0, at, cols].astype(F32)
@@ -415,7 +420,7 @@
             pltpu.VMEM((2, modes, 8, LANES), F32),
             pltpu.VMEM((2, 8, LANES), F32),
             pltpu.VMEM((2, waves, 8, LANES), F32),
-            dma((3,)),
+            dma((6,)),
             dma((2, CUTS)),
             dma((2, CUTS)),
             dma((2, CUTS, chips)),
@@ -434,7 +439,7 @@
             dma((2, waves)),
         ],
         compiler_params=pltpu.CompilerParams(
-            collective_id=0, has_side_effects=True, vmem_limit_bytes=56 * 1024 * 1024
+            collective_id=0, has_side_effects=True, vmem_limit_bytes=48 * 1024 * 1024
         ),
         cost_estimate=pl.CostEstimate(flops=16 * count**3 * 2, bytes_accessed=12 * count**2, transcendentals=0),
     )(scales, field_in[0, 0], target[0, 0], mask_old)

time: 57.7 us -> 62.2 us (1.078)
  local copies, waits for them, and re-layouts: 2.26 us -> 4.98 us
  Pallas kernels: 54 us -> 55.7 us
    unnamed x4 -> x8, local copies, waits for them, and re-layouts: 2.26 us -> 4.98 us
    pallas_call x1, Pallas kernels: 54 us -> 55.7 us  [fused(): pl.pallas_call(functools.partial(kernel, modes, waves), out_shape=(out, o...]
where the time goes in v3:
time: 62.2 us; the launch traced here: 61.9 us
  Pallas kernels  55.7 us (90%)
  local copies, waits for them, and re-layouts  4.98 us (8%)
  between operations  1.3 us (2%)
    pallas_call x1, Pallas kernels, fused(): pl.pallas_call(functools.partial(kernel, modes, waves), out_shape=(out, o...  55.7 us
    unnamed x8, local copies, waits for them, and re-layouts  4.98 us

profile of v3, /device:TPU:0, one launch (start us, length us, event | category | flops | bytes accessed | tf_op | source)
XLA Modules:
  0.0 61.9 jit_solution(5436122793346759184)
XLA Ops:
  1.3 0.0 copy-start
  1.3 1.2 %copy-done = bf16[1,1,2,512,512]{4,3,2,1,0:T(8,128)(2,1)S(1)} copy-done((bf16[1,1,2,512,512]{4,3,2,1,0:T(8,128)(2,1)S(1)}, bf16[1,1,2,512,512]{4,3,2,1,0:T(8,128)(2,1)}, u32[]{:S(2)}) %copy-start) | copy-done | bytes 1048600
  2.5 0.0 copy-start.1
  2.5 1.2 %copy-done.1 = bf16[1,1,2,512,512]{4,3,2,1,0:T(8,128)(2,1)S(1)} copy-done((bf16[1,1,2,512,512]{4,3,2,1,0:T(8,128)(2,1)S(1)}, bf16[1,1,2,512,512]{4,3,2,1,0:T(8,128)(2,1)}, u32[]{:S(2)}) %copy-start.1) | copy-done | bytes 1048600
  3.7 0.0 copy-start.2
  3.7 1.2 %copy-done.2 = bf16[2,512,512]{2,1,0:T(8,128)(2,1)S(1)} copy-done((bf16[2,512,512]{2,1,0:T(8,128)(2,1)S(1)}, bf16[2,512,512]{2,1,0:T(8,128)(2,1)}, u32[]{:S(2)}) %copy-start.2) | copy-done | bytes 1048600
  5.0 55.7 %shard_map.59 = (bf16[2,64,512]{2,1,0:T(8,128)(2,1)S(1)}, bf16[2,64,512]{2,1,0:T(8,128)(2,1)S(1)}) custom-call(f32[1]{0:T(128)S(6)} %copy.8.scale_ref, bf16[2,512,512]{2,1,0:T(8,128)(2,1)S(1)} %bitcast.2, bf16[2,512,512]{2,1,0:T(8,128)(2,1)S(1)} %bitcast.3, bf16[2,512,512]{2,1,0:T(8,128)(2,1)S(1)} %copy-done.2), custom_call_target="tpu_custom_call" | custom-call | flops 4294967296 | bytes 3145728 | tf_op jit(solution)/shard_map/pallas_call | solution.py:399
  60.6 0.7 %copy.9 = bf16[2,64,512]{2,1,0:T(8,128)(2,1)} copy(bf16[2,64,512]{2,1,0:T(8,128)(2,1)S(1)} %get-tuple-element.4) | data formatting | bytes 262144
  61.3 0.7 %copy.10 = bf16[2,64,512]{2,1,0:T(8,128)(2,1)} copy(bf16[2,64,512]{2,1,0:T(8,128)(2,1)S(1)} %get-tuple-element.5) | data formatting | bytes 262144
Async XLA Ops:
  1.3 1.2 %copy-start = (bf16[1,1,2,512,512]{4,3,2,1,0:T(8,128)(2,1)S(1)}, bf16[1,1,2,512,512]{4,3,2,1,0:T(8,128)(2,1)}, u32[]{:S(2)}) copy-start(bf16[1,1,2,512,512]{4,3,2,1,0:T(8,128)(2,1)} %param.4) | copy-start | bytes 3145732
  2.5 1.2 %copy-start.1 = (bf16[1,1,2,512,512]{4,3,2,1,0:T(8,128)(2,1)S(1)}, bf16[1,1,2,512,512]{4,3,2,1,0:T(8,128)(2,1)}, u32[]{:S(2)}) copy-start(bf16[1,1,2,512,512]{4,3,2,1,0:T(8,128)(2,1)} %param.5) | copy-start | bytes 3145732
  3.7 1.2 %copy-start.2 = (bf16[2,512,512]{2,1,0:T(8,128)(2,1)S(1)}, bf16[2,512,512]{2,1,0:T(8,128)(2,1)}, u32[]{:S(2)}) copy-start(bf16[2,512,512]{2,1,0:T(8,128)(2,1)} %old_hbm.1) | copy-start | bytes 3145732

commit v4 on v3

--- a/solution.py
+++ b/solution.py
@@ -12,7 +12,7 @@
 BF16 = jnp.bfloat16
 SUB = 16
 LANES = 128
-CUTS = 1
+CUTS = 2
 
 
 def build_right(scale, right, count):
@@ -48,8 +48,7 @@
     field_hbm,
     target_hbm,
     old_hbm,
-    out_one,
-    out_two,
+    masks,
     field,
     target,
     old,
@@ -115,6 +114,15 @@
             barrier, inc=1, device_id={"wave": lax.rem(wave + step, waves)}, device_id_type=MESH
         )
 
+    def partner(me, size, step):
+        if size == 4:
+            high, low = ((1, 1), (1, 0), (0, 1))[step - 1]
+            to = 2 * lax.rem(lax.div(me, 2) + high, 2) + lax.rem(lax.rem(me, 2) + low, 2)
+            return to, to
+        return lax.rem(me + step, size), lax.rem(me - step + size, size)
+
+    chip_to = [partner(chip, chips, step) for step in range(1, chips)]
+    wave_to = [partner(wave, waves, step) for step in range(1, waves)]
     pending = []
 
     def send(src, dst, s_sem, r_sem, to):
@@ -128,16 +136,18 @@
     def starts_of(which):
         return [pl.multiple_of((2 * q + which) * rows, rows) for q in range(chips)]
 
-    def right_rows(low, starts):
+    def right_rows(low, starts, cut):
         size = rows * len(starts)
         for half, base in ((0, count), (1, 0)):
             result = jnp.dot(
                 joined[pl.ds(low, size), :],
-                right[:, pl.ds(half * count, count)],
+                right[:, pl.ds(half * count + cut * width, width)],
                 preferred_element_type=F32,
             ).astype(BF16)
             for q, start in enumerate(starts):
-                middle[pl.ds(pl.multiple_of(base + start, rows), rows), :] = result[q * rows : (q + 1) * rows]
+                middle[pl.ds(pl.multiple_of(base + start, rows), rows), pl.ds(cut * width, width)] = result[
+                    q * rows : (q + 1) * rows
+                ]
 
     def left_half(trip, cut, which, term):
         starts = starts_of(which)
@@ -155,24 +165,28 @@
             part[trip, cut, which, q, :, pl.ds(0, width)] = term_re.astype(BF16)
             part[trip, cut, which, q, :, pl.ds(width, width)] = term_im.astype(BF16)
 
-    def reduce_scatter(trip, term, ready, arrived):
-        fans = []
+    def reduce_scatter(trip, prepare, term, ready, arrived):
+        crossings = []
         for cut in range(CUTS):
+            prepare(cut)
             left_half(trip, cut, other, term)
             if cut == 0:
                 ready()
-            crossing = send(
-                part.at[trip, cut, other],
-                core_in.at[trip, cut],
-                core_s.at[trip, cut],
-                core_r.at[trip, cut],
-                {"mode": 2 * chip + other},
+            crossings.append(
+                send(
+                    part.at[trip, cut, other],
+                    core_in.at[trip, cut],
+                    core_s.at[trip, cut],
+                    core_r.at[trip, cut],
+                    {"mode": 2 * chip + other},
+                )
             )
+        fans = []
+        for cut in range(CUTS):
             left_half(trip, cut, core, term)
-            crossing.wait_recv()
+            crossings[cut].wait_recv()
             fan = []
-            for step in range(1, chips):
-                to = lax.rem(chip + step, chips)
+            for step, (to, _) in enumerate(chip_to, 1):
                 chip_out[trip, cut, step] = (
                     part[trip, cut, core, to].astype(F32) + core_in[trip, cut, to].astype(F32)
                 ).astype(BF16)
@@ -194,8 +208,7 @@
                 total = total + chip_in[trip, cut, step].astype(F32)
             wave_out[trip, cut] = total.astype(BF16).reshape(waves, piece, 2 * width)
             hop = []
-            for step in range(1, waves):
-                to = lax.rem(wave + step, waves)
+            for step, (to, _) in enumerate(wave_to, 1):
                 hop.append(
                     send(
                         wave_out.at[trip, cut, to],
@@ -271,14 +284,18 @@
     o_im = old[1].astype(F32)
     joined[:, pl.ds(0, count)] = (t_re * o_re + t_im * o_im).astype(BF16)
     joined[:, pl.ds(count, count)] = (t_re * o_im - t_im * o_re).astype(BF16)
-    right_rows(0, [q * rows for q in range(modes)])
-    for copy in loads[4:]:
-        copy.wait()
+    every = [q * rows for q in range(modes)]
 
     def term_one(re, im, at, cols):
         f_re = field[0, at, cols].astype(F32)
         f_im = field[1, at, cols].astype(F32)
         return re * f_re - im * f_im, -(re * f_im + im * f_re)
+
+    def backward_right(cut):
+        right_rows(0, every, cut)
+        if cut == 0:
+            for copy in loads[4:]:
+                copy.wait()
 
     def entered():
         pl.semaphore_wait(barrier, modes - 1 + waves - 1)
@@ -296,18 +313,25 @@
                     own,
                     gw_s.at[trip, cut, step],
                     gw_r.at[trip, cut, step],
-                    {"wave": lax.rem(wave + step, waves)},
+                    {"wave": to},
                 )
-                for step in range(1, waves)
+                for step, (to, _) in enumerate(wave_to, 1)
             ]
         )
         squares.append(folded(value))
 
-    reduce_scatter(0, term_one, entered, lambda cut, v: spread(0, cut, whole.at[cut, core, chip, mine], v))
+    reduce_scatter(
+        0,
+        backward_right,
+        term_one,
+        entered,
+        lambda cut, v: spread(0, cut, whole.at[cut, core, chip, mine], v),
+    )
     tile = sum(squares[1:], squares[0])
     tiles = power_over_modes(0, tile)
     fans = []
     across = []
+    order = []
     for cut in range(CUTS):
         for copy in hops[cut]:
             copy.wait_recv()
@@ -319,41 +343,50 @@
                     block,
                     gx_s.at[cut, step],
                     gx_r.at[cut, step],
-                    {"mode": 2 * lax.rem(chip + step, chips) + core},
+                    {"mode": 2 * to + core},
                 )
-                for step in range(1, chips)
+                for step, (to, _) in enumerate(chip_to, 1)
             ]
         )
         across.append(send(block, block, gc_s.at[cut, 0], gc_r.at[cut, 0], {"mode": 2 * chip + other}))
+        order.append((cut, 0))
     tile, tiles2 = power_over_waves(0, tile, tiles)
+    sources = [chip] + [source for _, source in chip_to]
     for cut in range(CUTS):
         for step, copy in enumerate(fans[cut], 1):
             copy.wait_recv()
-            came = whole.at[cut, core, lax.rem(chip - step + chips, chips)]
+            came = whole.at[cut, core, sources[step]]
             across.append(
                 send(came, came, gc_s.at[cut, step], gc_r.at[cut, step], {"mode": 2 * chip + other})
             )
+            order.append((cut, step))
     power = mean_power(0, tile, tiles2)
 
-    def forward_half(which, low):
-        starts = starts_of(which)
-        for q, start in enumerate(starts):
-            at = pl.ds(low + q * rows, rows)
-            for cut in range(CUTS):
-                cols = pl.ds(cut * width, width)
-                m_re, m_im = phasor(whole[cut, which, q], power)
-                n_re = m_re.astype(F32)
-                n_im = m_im.astype(F32)
-                f_re = field[0, pl.ds(start, rows), cols].astype(F32)
-                f_im = field[1, pl.ds(start, rows), cols].astype(F32)
-                joined[at, cols] = (f_re * n_re - f_im * n_im).astype(BF16)
-                joined[at, pl.ds(count + cut * width, width)] = (f_re * n_im + f_im * n_re).astype(BF16)
-        right_rows(low, starts)
-
-    forward_half(core, 0)
-    for copy in across:
+    def masked(cut, which, source, at):
+        start = pl.multiple_of((2 * source + which) * rows, rows)
+        cols = pl.ds(cut * width, width)
+        m_re, m_im = phasor(whole[cut, which, source], power)
+        n_re = m_re.astype(F32)
+        n_im = m_im.astype(F32)
+        f_re = field[0, pl.ds(start, rows), cols].astype(F32)
+        f_im = field[1, pl.ds(start, rows), cols].astype(F32)
+        joined[at, cols] = (f_re * n_re - f_im * n_im).astype(BF16)
+        joined[at, pl.ds(count + cut * width, width)] = (f_re * n_im + f_im * n_re).astype(BF16)
+
+    def places(which):
+        return [pl.multiple_of((2 * source + which) * rows, rows) for source in sources]
+
+    for step, source in enumerate(sources):
+        for cut in range(CUTS):
+            masked(cut, core, source, pl.ds(step * rows, rows))
+    for cut in range(CUTS):
+        right_rows(0, places(core), cut)
+    for copy, (cut, step) in zip(across, order):
         copy.wait_recv()
-    forward_half(other, count // 2)
+        masked(cut, other, sources[step], pl.ds(count // 2 + step * rows, rows))
+
+    def forward_right(cut):
+        right_rows(count // 2, places(other), cut)
 
     def term_two(re, im, at, cols):
         b_re = target[0, at, cols].astype(F32)
@@ -362,14 +395,20 @@
 
     squares.clear()
     hops.clear()
-    reduce_scatter(1, term_two, lambda: None, lambda cut, v: spread(1, cut, last.at[cut, mine], v))
+    reduce_scatter(
+        1,
+        forward_right,
+        term_two,
+        lambda: None,
+        lambda cut, v: spread(1, cut, last.at[cut, mine], v),
+    )
     tile = sum(squares[1:], squares[0])
     tiles = power_over_modes(1, tile)
     for cut in range(CUTS):
         cols = pl.ds(cut * width, width)
         m_re, m_im = phasor(whole[cut, core, chip], power)
-        out_one[0, :, cols] = m_re
-        out_one[1, :, cols] = m_im
+        masks[0, :, cols] = m_re
+        masks[1, :, cols] = m_im
     tile, tiles2 = power_over_waves(1, tile, tiles)
     for hop in hops:
         for copy in hop:
@@ -378,8 +417,8 @@
     for cut in range(CUTS):
         cols = pl.ds(cut * width, width)
         m_re, m_im = phasor(last[cut], power)
-        out_two[0, :, cols] = m_re
-        out_two[1, :, cols] = m_im
+        masks[2, :, cols] = m_re
+        masks[3, :, cols] = m_im
     for copy in pending:
         copy.wait_send()
 
@@ -393,14 +432,14 @@
     piece = rows // waves
     wide = 2 * count // CUTS
     dma = pltpu.SemaphoreType.DMA
-    out = jax.ShapeDtypeStruct((2, rows, count), BF16)
+    out = jax.ShapeDtypeStruct((4, rows, count), BF16)
     vmem = pl.BlockSpec(memory_space=pltpu.VMEM)
     anywhere = pl.BlockSpec(memory_space=pl.ANY)
-    return pl.pallas_call(
+    masks = pl.pallas_call(
         functools.partial(kernel, modes, waves),
-        out_shape=(out, out),
+        out_shape=out,
         in_specs=[pl.BlockSpec(memory_space=pltpu.SMEM), anywhere, anywhere, anywhere],
-        out_specs=(vmem, vmem),
+        out_specs=vmem,
         scratch_shapes=[
             pltpu.VMEM((2, count, count), BF16),
             pltpu.VMEM((2, count, count), BF16),
@@ -439,10 +478,11 @@
             dma((2, waves)),
         ],
         compiler_params=pltpu.CompilerParams(
-            collective_id=0, has_side_effects=True, vmem_limit_bytes=48 * 1024 * 1024
+            collective_id=0, has_side_effects=True, vmem_limit_bytes=56 * 1024 * 1024
         ),
         cost_estimate=pl.CostEstimate(flops=16 * count**3 * 2, bytes_accessed=12 * count**2, transcendentals=0),
     )(scales, field_in[0, 0], target[0, 0], mask_old)
+    return masks[:2], masks[2:]
 
 
 def chirp(scale, count):

time: 62.2 us -> 56.8 us (0.913)
  local copies, waits for them, and re-layouts: 4.98 us -> 1.68 us
  Pallas kernels: 55.7 us -> 53.6 us
    unnamed x8 -> x0, local copies, waits for them, and re-layouts: 4.98 us -> none
    pallas_call x1, Pallas kernels: 55.7 us -> 53.6 us  [fused(): pl.pallas_call(functools.partial(kernel, modes, waves), out_shape=out, in...]
    slice x0 -> x1, local copies, waits for them, and re-layouts: none -> 1.68 us  [fused(): return (masks[:2], masks[2:])]
where the time goes in v4:
time: 56.8 us; the launch traced here: 56.6 us
  Pallas kernels  53.6 us (94%)
  local copies, waits for them, and re-layouts  1.68 us (3%)
  between operations  1.29 us (2%)
    pallas_call x1, Pallas kernels, fused(): pl.pallas_call(functools.partial(kernel, modes, waves), out_shape=out, in...  53.6 us
    slice x1, local copies, waits for them, and re-layouts, fused(): return (masks[:2], masks[2:])  1.68 us

profile of v4, /device:TPU:0, one launch (start us, length us, event | category | flops | bytes accessed | tf_op | source)
XLA Modules:
  0.0 56.6 jit_solution(14404145806946182105)
XLA Ops:
  1.3 53.6 %shard_map.59 = bf16[4,64,512]{2,1,0:T(8,128)(2,1)} custom-call(f32[1]{0:T(128)S(6)} %copy.6.scale_ref, bf16[2,512,512]{2,1,0:T(8,128)(2,1)} %bitcast.2, bf16[2,512,512]{2,1,0:T(8,128)(2,1)} %bitcast.3, bf16[2,512,512]{2,1,0:T(8,128)(2,1)} %old_hbm.1), custom_call_target="tpu_custom_call" | custom-call | flops 4294967296 | bytes 3145728 | tf_op jit(solution)/shard_map/pallas_call | solution.py:438
  54.9 1.7 %fusion = (bf16[2,64,512]{2,1,0:T(8,128)(2,1)}, bf16[2,64,512]{2,1,0:T(8,128)(2,1)}) fusion(bf16[4,64,512]{2,1,0:T(8,128)(2,1)} %shard_map.59), kind=kLoop, calls=%fused_computation | loop fusion | bytes 524288 | tf_op jit(solution)/shard_map/slice | solution.py:485

commit v5 on v4

--- a/solution.py
+++ b/solution.py
@@ -114,15 +114,16 @@
             barrier, inc=1, device_id={"wave": lax.rem(wave + step, waves)}, device_id_type=MESH
         )
 
-    def partner(me, size, step):
+    def partner(me, size, step, turns):
         if size == 4:
-            high, low = ((1, 1), (1, 0), (0, 1))[step - 1]
+            high, low = turns[step - 1]
             to = 2 * lax.rem(lax.div(me, 2) + high, 2) + lax.rem(lax.rem(me, 2) + low, 2)
             return to, to
         return lax.rem(me + step, size), lax.rem(me - step + size, size)
 
-    chip_to = [partner(chip, chips, step) for step in range(1, chips)]
-    wave_to = [partner(wave, waves, step) for step in range(1, waves)]
+    chip_to = [partner(chip, chips, step, ((core, other), (other, core), (1, 1))) for step in range(1, chips)]
+    other_to = [partner(chip, chips, step, ((other, core), (core, other), (1, 1))) for step in range(1, chips)]
+    wave_to = [partner(wave, waves, step, ((1, 0), (1, 1), (0, 1))) for step in range(1, waves)]
     pending = []
 
     def send(src, dst, s_sem, r_sem, to):
@@ -352,6 +353,7 @@
         order.append((cut, 0))
     tile, tiles2 = power_over_waves(0, tile, tiles)
     sources = [chip] + [source for _, source in chip_to]
+    others = [chip] + [source for _, source in other_to]
     for cut in range(CUTS):
         for step, copy in enumerate(fans[cut], 1):
             copy.wait_recv()
@@ -373,20 +375,20 @@
         joined[at, cols] = (f_re * n_re - f_im * n_im).astype(BF16)
         joined[at, pl.ds(count + cut * width, width)] = (f_re * n_im + f_im * n_re).astype(BF16)
 
-    def places(which):
-        return [pl.multiple_of((2 * source + which) * rows, rows) for source in sources]
+    def places(which, chain):
+        return [pl.multiple_of((2 * source + which) * rows, rows) for source in chain]
 
     for step, source in enumerate(sources):
         for cut in range(CUTS):
             masked(cut, core, source, pl.ds(step * rows, rows))
     for cut in range(CUTS):
-        right_rows(0, places(core), cut)
+        right_rows(0, places(core, sources), cut)
     for copy, (cut, step) in zip(across, order):
         copy.wait_recv()
-        masked(cut, other, sources[step], pl.ds(count // 2 + step * rows, rows))
+        masked(cut, other, others[step], pl.ds(count // 2 + step * rows, rows))
 
     def forward_right(cut):
-        right_rows(count // 2, places(other), cut)
+        right_rows(count // 2, places(other, others), cut)
 
     def term_two(re, im, at, cols):
         b_re = target[0, at, cols].astype(F32)

time: 56.8 us -> 56.7 us (level)
  no operation moved by 1% of the time
where the time goes in v5:
time: 56.7 us; the launch traced here: 56.5 us
  Pallas kernels  53.6 us (95%)
  local copies, waits for them, and re-layouts  1.68 us (3%)
  between operations  1.29 us (2%)
    pallas_call x1, Pallas kernels, fused(): pl.pallas_call(functools.partial(kernel, modes, waves), out_shape=out, in...  53.6 us
    slice x1, local copies, waits for them, and re-layouts, fused(): return (masks[:2], masks[2:])  1.68 us

profile of v5, /device:TPU:0, one launch (start us, length us, event | category | flops | bytes accessed | tf_op | source)
XLA Modules:
  0.0 56.5 jit_solution(15253838150360721210)
XLA Ops:
  1.3 53.6 %shard_map.59 = bf16[4,64,512]{2,1,0:T(8,128)(2,1)} custom-call(f32[1]{0:T(128)S(6)} %copy.6.scale_ref, bf16[2,512,512]{2,1,0:T(8,128)(2,1)} %bitcast.2, bf16[2,512,512]{2,1,0:T(8,128)(2,1)} %bitcast.3, bf16[2,512,512]{2,1,0:T(8,128)(2,1)} %old_hbm.1), custom_call_target="tpu_custom_call" | custom-call | flops 4294967296 | bytes 3145728 | tf_op jit(solution)/shard_map/pallas_call | solution.py:440
  54.9 1.7 %fusion = (bf16[2,64,512]{2,1,0:T(8,128)(2,1)}, bf16[2,64,512]{2,1,0:T(8,128)(2,1)}) fusion(bf16[4,64,512]{2,1,0:T(8,128)(2,1)} %shard_map.59), kind=kLoop, calls=%fused_computation | loop fusion | bytes 524288 | tf_op jit(solution)/shard_map/slice | solution.py:487

commit v6 on v5

--- a/solution.py
+++ b/solution.py
@@ -201,30 +201,28 @@
                     )
                 )
             fans.append(fan)
-        hops = []
         for cut in range(CUTS):
             total = part[trip, cut, core, chip].astype(F32) + core_in[trip, cut, chip].astype(F32)
             for step, copy in enumerate(fans[cut], 1):
                 copy.wait_recv()
                 total = total + chip_in[trip, cut, step].astype(F32)
-            wave_out[trip, cut] = total.astype(BF16).reshape(waves, piece, 2 * width)
-            hop = []
-            for step, (to, _) in enumerate(wave_to, 1):
-                hop.append(
-                    send(
-                        wave_out.at[trip, cut, to],
-                        wave_in.at[trip, cut, step],
-                        wave_s.at[trip, cut, step],
-                        wave_r.at[trip, cut, step],
-                        {"wave": to},
-                    )
-                )
-            hops.append(hop)
+            wave_out[trip, :, cut] = total.astype(BF16).reshape(waves, piece, 2 * width)
+        hops = [
+            send(
+                wave_out.at[trip, to],
+                wave_in.at[trip, step],
+                wave_s.at[trip, step],
+                wave_r.at[trip, step],
+                {"wave": to},
+            )
+            for step, (to, _) in enumerate(wave_to, 1)
+        ]
+        for copy in hops:
+            copy.wait_recv()
         for cut in range(CUTS):
-            result = wave_out[trip, cut, wave].astype(F32)
-            for step, copy in enumerate(hops[cut], 1):
-                copy.wait_recv()
-                result = result + wave_in[trip, cut, step].astype(F32)
+            result = wave_out[trip, wave, cut].astype(F32)
+            for step in range(1, waves):
+                result = result + wave_in[trip, step, cut].astype(F32)
             arrived(cut, result)
 
     def folded(values):
@@ -303,65 +301,42 @@
 
     mine = pl.ds(pl.multiple_of(wave * piece, piece), piece)
     squares = []
-    hops = []
-
-    def spread(trip, cut, own, value):
-        own[...] = value.astype(BF16)
-        hops.append(
-            [
-                send(
-                    own,
-                    own,
-                    gw_s.at[trip, cut, step],
-                    gw_r.at[trip, cut, step],
-                    {"wave": to},
-                )
-                for step, (to, _) in enumerate(wave_to, 1)
-            ]
-        )
+
+    def keep(own, cut, value):
+        own[cut] = value.astype(BF16)
         squares.append(folded(value))
+
+    def spread(trip, own):
+        return [
+            send(own, own, gw_s.at[trip, step], gw_r.at[trip, step], {"wave": to})
+            for step, (to, _) in enumerate(wave_to, 1)
+        ]
 
     reduce_scatter(
         0,
         backward_right,
         term_one,
         entered,
-        lambda cut, v: spread(0, cut, whole.at[cut, core, chip, mine], v),
-    )
+        lambda cut, v: keep(whole.at[:, core, chip, mine], cut, v),
+    )
+    hops = spread(0, whole.at[:, core, chip, mine])
     tile = sum(squares[1:], squares[0])
     tiles = power_over_modes(0, tile)
-    fans = []
-    across = []
-    order = []
-    for cut in range(CUTS):
-        for copy in hops[cut]:
-            copy.wait_recv()
-        block = whole.at[cut, core, chip]
-        fans.append(
-            [
-                send(
-                    block,
-                    block,
-                    gx_s.at[cut, step],
-                    gx_r.at[cut, step],
-                    {"mode": 2 * to + core},
-                )
-                for step, (to, _) in enumerate(chip_to, 1)
-            ]
-        )
-        across.append(send(block, block, gc_s.at[cut, 0], gc_r.at[cut, 0], {"mode": 2 * chip + other}))
-        order.append((cut, 0))
+    for copy in hops:
+        copy.wait_recv()
+    block = whole.at[:, core, chip]
+    fan = [
+        send(block, block, gx_s.at[step], gx_r.at[step], {"mode": 2 * to + core})
+        for step, (to, _) in enumerate(chip_to, 1)
+    ]
+    across = [send(block, block, gc_s.at[0], gc_r.at[0], {"mode": 2 * chip + other})]
     tile, tiles2 = power_over_waves(0, tile, tiles)
     sources = [chip] + [source for _, source in chip_to]
     others = [chip] + [source for _, source in other_to]
-    for cut in range(CUTS):
-        for step, copy in enumerate(fans[cut], 1):
-            copy.wait_recv()
-            came = whole.at[cut, core, sources[step]]
-            across.append(
-                send(came, came, gc_s.at[cut, step], gc_r.at[cut, step], {"mode": 2 * chip + other})
-            )
-            order.append((cut, step))
+    for step, copy in enumerate(fan, 1):
+        copy.wait_recv()
+        came = whole.at[:, core, sources[step]]
+        across.append(send(came, came, gc_s.at[step], gc_r.at[step], {"mode": 2 * chip + other}))
     power = mean_power(0, tile, tiles2)
 
     def masked(cut, which, source, at):
@@ -383,9 +358,10 @@
             masked(cut, core, source, pl.ds(step * rows, rows))
     for cut in range(CUTS):
         right_rows(0, places(core, sources), cut)
-    for copy, (cut, step) in zip(across, order):
+    for step, copy in enumerate(across):
         copy.wait_recv()
-        masked(cut, other, others[step], pl.ds(count // 2 + step * rows, rows))
+        for cut in range(CUTS):
+            masked(cut, other, others[step], pl.ds(count // 2 + step * rows, rows))
 
     def forward_right(cut):
         right_rows(count // 2, places(other, others), cut)
@@ -396,25 +372,24 @@
         return b_re * re + b_im * im, b_im * re - b_re * im
 
     squares.clear()
-    hops.clear()
     reduce_scatter(
         1,
         forward_right,
         term_two,
         lambda: None,
-        lambda cut, v: spread(1, cut, last.at[cut, mine], v),
+        lambda cut, v: keep(last.at[:, mine], cut, v),
     )
     tile = sum(squares[1:], squares[0])
     tiles = power_over_modes(1, tile)
+    hops = spread(1, last.at[:, mine])
     for cut in range(CUTS):
         cols = pl.ds(cut * width, width)
         m_re, m_im = phasor(whole[cut, core, chip], power)
         masks[0, :, cols] = m_re
         masks[1, :, cols] = m_im
     tile, tiles2 = power_over_waves(1, tile, tiles)
-    for hop in hops:
-        for copy in hop:
-            copy.wait_recv()
+    for copy in hops:
+        copy.wait_recv()
     power = mean_power(1, tile, tiles2)
     for cut in range(CUTS):
         cols = pl.ds(cut * width, width)
@@ -453,8 +428,8 @@
             pltpu.VMEM((2, CUTS, chips, rows, wide), BF16),
             pltpu.VMEM((2, CUTS, chips, rows, wide), BF16),
             pltpu.VMEM((2, CUTS, chips, rows, wide), BF16),
-            pltpu.VMEM((2, CUTS, waves, piece, wide), BF16),
-            pltpu.VMEM((2, CUTS, waves, piece, wide), BF16),
+            pltpu.VMEM((2, waves, CUTS, piece, wide), BF16),
+            pltpu.VMEM((2, waves, CUTS, piece, wide), BF16),
             pltpu.VMEM((CUTS, 2, chips, rows, wide), BF16),
             pltpu.VMEM((CUTS, rows, wide), BF16),
             pltpu.VMEM((2, 8, LANES), F32),
@@ -466,14 +441,14 @@
             dma((2, CUTS)),
             dma((2, CUTS, chips)),
             dma((2, CUTS, chips)),
-            dma((2, CUTS, waves)),
-            dma((2, CUTS, waves)),
-            dma((2, CUTS, waves)),
-            dma((2, CUTS, waves)),
-            dma((CUTS, chips)),
-            dma((CUTS, chips)),
-            dma((CUTS, chips)),
-            dma((CUTS, chips)),
+            dma((2, waves)),
+            dma((2, waves)),
+            dma((2, waves)),
+            dma((2, waves)),
+            dma((chips,)),
+            dma((chips,)),
+            dma((chips,)),
+            dma((chips,)),
             dma((2, modes)),
             dma((2, modes)),
             dma((2, waves)),

time: 56.7 us -> 59.3 us (1.046)
  Pallas kernels: 53.6 us -> 56.1 us
    pallas_call x1, Pallas kernels: 53.6 us -> 56.1 us  [fused(): pl.pallas_call(functools.partial(kernel, modes, waves), out_shape=out, in...]
where the time goes in v6:
time: 59.3 us; the launch traced here: 59.1 us
  Pallas kernels  56.1 us (95%)
  local copies, waits for them, and re-layouts  1.68 us (3%)
  between operations  1.29 us (2%)
    pallas_call x1, Pallas kernels, fused(): pl.pallas_call(functools.partial(kernel, modes, waves), out_shape=out, in...  56.1 us
    slice x1, local copies, waits for them, and re-layouts, fused(): return (masks[:2], masks[2:])  1.68 us

profile of v6, /device:TPU:0, one launch (start us, length us, event | category | flops | bytes accessed | tf_op | source)
XLA Modules:
  0.0 59.1 jit_solution(2001645857596622562)
XLA Ops:
  1.3 56.1 %shard_map.59 = bf16[4,64,512]{2,1,0:T(8,128)(2,1)} custom-call(f32[1]{0:T(128)S(6)} %copy.6.scale_ref, bf16[2,512,512]{2,1,0:T(8,128)(2,1)} %bitcast.2, bf16[2,512,512]{2,1,0:T(8,128)(2,1)} %bitcast.3, bf16[2,512,512]{2,1,0:T(8,128)(2,1)} %old_hbm.1), custom_call_target="tpu_custom_call" | custom-call | flops 4294967296 | bytes 3145728 | tf_op jit(solution)/shard_map/pallas_call | solution.py:415
  57.4 1.7 %fusion = (bf16[2,64,512]{2,1,0:T(8,128)(2,1)}, bf16[2,64,512]{2,1,0:T(8,128)(2,1)}) fusion(bf16[4,64,512]{2,1,0:T(8,128)(2,1)} %shard_map.59), kind=kLoop, calls=%fused_computation | loop fusion | bytes 524288 | tf_op jit(solution)/shard_map/slice | solution.py:462

commit v7 on v5

--- a/solution.py
+++ b/solution.py
@@ -12,7 +12,7 @@
 BF16 = jnp.bfloat16
 SUB = 16
 LANES = 128
-CUTS = 2
+CUTS = 4
 
 
 def build_right(scale, right, count):

time: 56.7 us -> 62.9 us (1.11)
  Pallas kernels: 53.6 us -> 59.8 us
    pallas_call x1, Pallas kernels: 53.6 us -> 59.8 us  [fused(): pl.pallas_call(functools.partial(kernel, modes, waves), out_shape=out, in...]
where the time goes in v7:
time: 62.9 us; the launch traced here: 62.7 us
  Pallas kernels  59.8 us (95%)
  local copies, waits for them, and re-layouts  1.68 us (3%)
  between operations  1.29 us (2%)
    pallas_call x1, Pallas kernels, fused(): pl.pallas_call(functools.partial(kernel, modes, waves), out_shape=out, in...  59.8 us
    slice x1, local copies, waits for them, and re-layouts, fused(): return (masks[:2], masks[2:])  1.68 us

profile of v7, /device:TPU:0, one launch (start us, length us, event | category | flops | bytes accessed | tf_op | source)
XLA Modules:
  0.0 62.7 jit_solution(15368024724931747261)
XLA Ops:
  1.3 59.8 %shard_map.59 = bf16[4,64,512]{2,1,0:T(8,128)(2,1)} custom-call(f32[1]{0:T(128)S(6)} %copy.6.scale_ref, bf16[2,512,512]{2,1,0:T(8,128)(2,1)} %bitcast.2, bf16[2,512,512]{2,1,0:T(8,128)(2,1)} %bitcast.3, bf16[2,512,512]{2,1,0:T(8,128)(2,1)} %old_hbm.1), custom_call_target="tpu_custom_call" | custom-call | flops 4294967296 | bytes 3145728 | tf_op jit(solution)/shard_map/pallas_call | solution.py:440
  61.0 1.7 %fusion = (bf16[2,64,512]{2,1,0:T(8,128)(2,1)}, bf16[2,64,512]{2,1,0:T(8,128)(2,1)}) fusion(bf16[4,64,512]{2,1,0:T(8,128)(2,1)} %shard_map.59), kind=kLoop, calls=%fused_computation | loop fusion | bytes 524288 | tf_op jit(solution)/shard_map/slice | solution.py:487
